TPU v7x, 256 devices: a whole 4x4x8 slice. The times are simulated.
256 devices in a mesh: row: 16 (over x, y_hi, core), col: 16 (over y_lo, z).
Axes of the slice: x: 4, y: 4 (y_hi: 2, y_lo: 2; y = y_hi * 2 + y_lo), z: 8, core: 2. Of those that a mesh axis runs over, the one named last changes fastest.
Arguments:
- pair_out: bfloat16 [512, 768, 128], P('row', 'col'), may hold values from -6 to 6
- pair_left: bfloat16 [512, 512, 128], P('col', 'row'), may hold values from -6 to 6
- pair_right: bfloat16 [512, 768, 128], P('row', 'col'), may hold values from -6 to 6
- ln_gain: float32 [128], replicated, may hold values from 0.1 to 1.9
- ln_bias: float32 [128], replicated, may hold values from -3 to 3
- w_left: bfloat16 [128, 256], replicated, may hold values from -0.5 to 0.5
- w_right: bfloat16 [128, 256], replicated, may hold values from -0.5 to 0.5
- w_gate: bfloat16 [128, 128], replicated, may hold values from -0.5 to 0.5
- w_out: bfloat16 [128, 128], replicated, may hold values from -0.5 to 0.5
- out_gain: float32 [128], replicated, may hold values from 0.1 to 1.9
- out_bias: float32 [128], replicated, may hold values from -3 to 3
- cotangent: bfloat16 [512, 768, 128], P('row', 'col'), may hold values from -6 to 6
Outputs:
- result: bfloat16 [512, 768, 128], P('row', 'col')
- grad_out: bfloat16 [512, 768, 128], P('row', 'col')
- grad_left: bfloat16 [512, 512, 128], P('col', 'row')
- grad_right: bfloat16 [512, 768, 128], P('row', 'col')
All inputs are finite; a program needn't handle non-finite values.
Results may differ from a plain program's by a relative error of at most 0.025.
Values may be sent and summed in bfloat16 or wider, within the bound.
A program may use at most 128 MiB of HBM per device.

v0:
```python
import jax
import jax.numpy as jnp
from jax import lax
from jax.sharding import PartitionSpec as P


def normalize(values, gain, bias):
    center = values - jnp.mean(values, axis=-1, keepdims=True)
    inverse = lax.rsqrt(jnp.mean(center * center, axis=-1, keepdims=True) + 1e-05)
    standard = center * inverse
    return (standard * gain + bias, standard, inverse)


def norm_back(upstream, standard, inverse, gain):
    scaled = upstream * gain
    return inverse * (
        scaled
        - jnp.mean(scaled, axis=-1, keepdims=True)
        - standard * jnp.mean(scaled * standard, axis=-1, keepdims=True)
    )


def project(pair_tile, gain, bias, weight):
    normed, standard, inverse = normalize(pair_tile.astype(jnp.float32), gain, bias)
    normed = normed.astype(jnp.bfloat16)
    hidden_width = weight.shape[1] // 2
    pre_act = jnp.dot(
        normed.reshape(-1, normed.shape[-1]), weight, preferred_element_type=jnp.float32
    )
    pre_act = pre_act.reshape(pair_tile.shape[:-1] + (2 * hidden_width,))
    gated = (jax.nn.sigmoid(pre_act[..., hidden_width:]) * pre_act[..., :hidden_width]).astype(
        jnp.bfloat16
    )
    return (gated, pre_act, standard, inverse)


def project_back(d_gated, pre_act, standard, inverse, gain, weight):
    hidden_width = weight.shape[1] // 2
    squash = jax.nn.sigmoid(pre_act[..., hidden_width:])
    values_half = pre_act[..., :hidden_width]
    d_pre = jnp.concatenate(
        [d_gated * squash, d_gated * values_half * squash * (1.0 - squash)], axis=-1
    )
    d_pre = d_pre.astype(jnp.bfloat16)
    d_normed = jnp.dot(
        d_pre.reshape(-1, 2 * hidden_width), weight.T, preferred_element_type=jnp.float32
    )
    return norm_back(d_normed.reshape(standard.shape), standard, inverse, gain).astype(jnp.bfloat16)


def per_device(
    pair_out,
    pair_left,
    pair_right,
    ln_gain,
    ln_bias,
    w_left,
    w_right,
    w_gate,
    w_out,
    out_gain,
    out_bias,
    cotangent,
):
    features = pair_out.shape[2]
    hidden_width = w_out.shape[0]
    left_gated, left_pre, left_std, left_inv = project(pair_left, ln_gain, ln_bias, w_left)
    right_gated, right_pre, right_std, right_inv = project(pair_right, ln_gain, ln_bias, w_right)
    left_full = lax.all_gather(left_gated, "col", axis=0, tiled=True)
    right_full = lax.all_gather(right_gated, "row", axis=0, tiled=True)
    triangle = jnp.einsum("kih,kjh->ijh", left_full, right_full, preferred_element_type=jnp.float32)
    tri_normed, tri_std, tri_inv = normalize(triangle, out_gain, out_bias)
    tri_normed = tri_normed.astype(jnp.bfloat16)
    out_normed, out_std, out_inv = normalize(pair_out.astype(jnp.float32), ln_gain, ln_bias)
    out_normed = out_normed.astype(jnp.bfloat16)
    out_gate = jax.nn.sigmoid(
        jnp.dot(out_normed.reshape(-1, features), w_gate, preferred_element_type=jnp.float32)
    )
    out_proj = jnp.dot(
        tri_normed.reshape(-1, hidden_width), w_out, preferred_element_type=jnp.float32
    )
    result = (out_gate * out_proj).astype(jnp.bfloat16).reshape(pair_out.shape)
    upstream = cotangent.reshape(-1, features).astype(jnp.float32)
    d_proj = (upstream * out_gate).astype(jnp.bfloat16)
    d_gate = (upstream * out_proj * out_gate * (1.0 - out_gate)).astype(jnp.bfloat16)
    d_outn = jnp.dot(d_gate, w_gate.T, preferred_element_type=jnp.float32).reshape(pair_out.shape)
    grad_out = norm_back(d_outn, out_std, out_inv, ln_gain).astype(jnp.bfloat16)
    d_trin = jnp.dot(d_proj, w_out.T, preferred_element_type=jnp.float32).reshape(triangle.shape)
    d_triangle = norm_back(d_trin, tri_std, tri_inv, out_gain).astype(jnp.bfloat16)
    d_left = lax.psum_scatter(
        jnp.einsum(
            "ijh,kjh->kih", d_triangle, right_full, preferred_element_type=jnp.float32
        ).astype(jnp.bfloat16),
        "col",
        scatter_dimension=0,
        tiled=True,
    ).astype(jnp.float32)
    d_right = lax.psum_scatter(
        jnp.einsum(
            "ijh,kih->kjh", d_triangle, left_full, preferred_element_type=jnp.float32
        ).astype(jnp.bfloat16),
        "row",
        scatter_dimension=0,
        tiled=True,
    ).astype(jnp.float32)
    grad_left = project_back(d_left, left_pre, left_std, left_inv, ln_gain, w_left)
    grad_right = project_back(d_right, right_pre, right_std, right_inv, ln_gain, w_right)
    return (result, grad_out, grad_left, grad_right)


def solution(mesh):
    return jax.shard_map(
        per_device,
        mesh=mesh,
        in_specs=(
            P("row", "col", None),
            P("col", "row", None),
            P("row", "col", None),
            P(),
            P(),
            P(),
            P(),
            P(),
            P(),
            P(),
            P(),
            P("row", "col", None),
        ),
        out_specs=(
            P("row", "col", None),
            P("row", "col", None),
            P("col", "row", None),
            P("row", "col", None),
        ),
        check_vma=False,
    )
```

profile of v0, /device:TPU:2, one launch (start us, length us, event | category | flops | bytes accessed | tf_op | source)
XLA Modules:
  0.0 410.6 jit_solution(10935491577532320342)
XLA Ops:
  7.2 1.2 convert_reduce_fusion.2
  8.5 1.3 fusion.53
  9.9 1.4 fusion.75
  11.3 1.0 copy-done.6
  12.3 0.8 multiply_convert_fusion.3
  13.2 0.3 convert_reduce_fusion
  13.5 0.5 fusion.20
  14.1 0.6 fusion.68
  14.7 1.1 copy-done.2
  15.8 1.0 multiply_convert_fusion.2
  16.8 0.2 reduce-scatter.3.cloned.1.call-start
  17.1 0.3 convert_reduce_fusion.1
  17.3 0.5 fusion.27
  17.9 0.5 fusion.22
  18.4 0.3 fusion.2
  18.8 0.9 copy-done.8
  19.6 0.5 multiply_reduce_fusion.2
  20.2 2.8 copy.34
  23.0 70.1 %all-gather.5.cloned.1.call-done = bf16[512,32,128]{2,1,0:T(8,128)(2,1)} async-done(((bf16[32,32,128]{2,1,0:T(8,128)(2,1)}), bf16[512,32,128]{2,1,0:T(8,128)(2,1)}) %all-gather.5.cloned.1.call-update) | async-done | bytes 4194320 | tf_op jit(solution)/shard_map/all_gather | solution.py:69
  93.1 23.0 %copy.37 = bf16[512,32,128]{1,0,2:T(8,128)(2,1)} copy(bf16[512,32,128]{2,1,0:T(8,128)(2,1)} %all-gather.5.cloned.1.call-done) | data formatting | bytes 8388608 | tf_op jit(solution)/shard_map/all_gather | solution.py:69
  116.2 46.3 %all-gather.3.cloned.1.call-done = bf16[512,48,128]{2,1,0:T(8,128)(2,1)} async-done(((bf16[32,48,128]{2,1,0:T(8,128)(2,1)}), bf16[512,48,128]{2,1,0:T(8,128)(2,1)}) %all-gather.3.cloned.1.call-update) | async-done | bytes 6291472 | tf_op jit(solution)/shard_map/all_gather | solution.py:70
  162.5 23.1 %copy.31 = bf16[512,48,128]{1,0,2:T(8,128)(2,1)} copy(bf16[512,48,128]{2,1,0:T(8,128)(2,1)} %all-gather.3.cloned.1.call-done) | data formatting | bytes 12582912 | tf_op jit(solution)/shard_map/all_gather | solution.py:70
  185.6 13.3 %bitcast_reduce_fusion = (f32[32,48]{1,0:T(8,128)S(1)}, f32[128,48,32]{1,2,0:T(8,128)S(1)}) fusion(bf16[512,32,128]{1,0,2:T(8,128)(2,1)} %copy.37, bf16[512,48,128]{1,0,2:T(8,128)(2,1)} %copy.31), kind=kOutput, calls=%fused_computation.7 | convolution fusion | flops 201521664 | bytes 11278336 | tf_op jit(solution)/shard_map/kih,kjh->ijh/dot_general | solution.py:71
  198.9 0.3 multiply_reduce_fusion.1
  199.3 1.2 copy-done.1
  200.5 0.4 multiply_reduce_fusion
  200.9 0.2 copy-done.22
  201.1 1.8 multiply_convert_fusion
  202.9 10.8 %fusion.90 = bf16[128,512,32]{1,2,0:T(8,128)(2,1)} fusion(bf16[512,48,128]{1,0,2:T(8,128)(2,1)} %copy.31, bf16[32,48,128]{1,0,2:T(8,128)(2,1)S(1)} %get-tuple-element.8), kind=kOutput, calls=%fused_computation.132 | convolution fusion | flops 201326592 | bytes 10878976 | tf_op jit(solution)/shard_map/ijh,kjh->kih/dot_general | solution.py:91
  213.7 9.1 %copy.36 = bf16[128,512,32]{0,2,1:T(8,128)(2,1)} copy(bf16[128,512,32]{1,2,0:T(8,128)(2,1)} %fusion.90) | data formatting | bytes 8388608 | tf_op jit(solution)/shard_map/ijh,kjh->kih/dot_general | solution.py:91
  222.8 0.3 reduce-scatter.5.cloned.1.call-start
  223.1 11.2 %fusion.91 = bf16[128,512,48]{1,2,0:T(8,128)(2,1)} fusion(bf16[512,32,128]{1,0,2:T(8,128)(2,1)} %copy.37, bf16[32,48,128]{1,0,2:T(8,128)(2,1)S(1)} %get-tuple-element.8), kind=kOutput, calls=%fused_computation.133 | convolution fusion | flops 201326592 | bytes 10878976 | tf_op jit(solution)/shard_map/ijh,kih->kjh/dot_general | solution.py:99
  234.3 9.8 %copy.38 = bf16[128,512,48]{0,2,1:T(8,128)(2,1)} copy(bf16[128,512,48]{1,2,0:T(8,128)(2,1)} %fusion.91) | data formatting | bytes 12582912 | tf_op jit(solution)/shard_map/ijh,kih->kjh/dot_general | solution.py:99
  244.2 1.2 copy-done.13
  245.4 1.1 copy.33
  246.5 1.0 multiply_convert_fusion.1
  247.5 0.5 multiply_reduce_fusion.3
  248.0 0.1 div.75
  248.1 0.7 fusion.23
  248.8 1.7 fusion.26
  250.5 51.9 %reduce-scatter.3.cloned.1.call-done = bf16[32,32,128]{2,1,0:T(8,128)(2,1)} async-done(((bf16[512,32,128]{2,1,0:T(8,128)(2,1)}), bf16[32,32,128]{2,1,0:T(8,128)(2,1)}) %reduce-scatter.3.cloned.1.call-update) | async-done | bytes 262160 | tf_op jit(solution)/shard_map/reduce_scatter | solution.py:90
  302.4 1.2 fusion.54
  303.6 0.8 fusion.89
  304.5 1.3 fusion.52
  305.8 94.3 %reduce-scatter.5.cloned.1.call-done = bf16[32,48,128]{2,1,0:T(8,128)(2,1)} async-done(((bf16[512,48,128]{2,1,0:T(8,128)(2,1)}), bf16[32,48,128]{2,1,0:T(8,128)(2,1)}) %reduce-scatter.5.cloned.1.call-update) | async-done | bytes 393232 | tf_op jit(solution)/shard_map/reduce_scatter | solution.py:98
  400.1 1.3 fusion.28
  401.5 0.9 fusion.88
  402.4 1.7 fusion.19
  (61 shorter events, 0.4 us)
Async XLA Ops:
  7.2 6.9 %copy-start = (bf16[128,256]{1,0:T(8,128)(2,1)S(1)}, bf16[128,256]{1,0:T(8,128)(2,1)}, u32[]{:S(2)}) copy-start(bf16[128,256]{1,0:T(8,128)(2,1)} %param.18) | copy-start | bytes 196612
  7.2 6.0 %copy-start.10 = (bf16[32,48,128]{2,1,0:T(8,128)(2,1)S(1)}, bf16[32,48,128]{2,1,0:T(8,128)(2,1)}, u32[]{:S(2)}) copy-start(bf16[32,48,128]{2,1,0:T(8,128)(2,1)} %param.14) | copy-start | bytes 1179652
  7.2 85.9 %all-gather.5.cloned.1.call-start = ((), (), s32[]{:S(2)}) async-start(), calls=%async_computation.3 | async-start | bytes 4456448 | tf_op jit(solution)/shard_map/all_gather | solution.py:69
  8.5 5.6 %copy-start.19 = (f32[128]{0:T(128)S(1)}, f32[128]{0:T(128)}, u32[]{:S(2)}) copy-start(f32[128]{0:T(128)} %param.15) | copy-start | bytes 1540
  8.5 5.6 %copy-start.20 = (f32[128]{0:T(128)S(1)}, f32[128]{0:T(128)}, u32[]{:S(2)}) copy-start(f32[128]{0:T(128)} %param.16) | copy-start | bytes 1540
  11.3 1.0 copy-start.6
  13.2 149.3 %all-gather.3.cloned.1.call-start = ((), (), s32[]{:S(2)}) async-start(), calls=%async_computation.2 | async-start | bytes 6684672 | tf_op jit(solution)/shard_map/all_gather | solution.py:70
  14.1 3.0 copy-start.4
  14.7 1.2 copy-start.2
  15.8 2.6 copy-start.18
  16.8 285.6 %reduce-scatter.3.cloned.1.call-start = ((), (), s32[]{:S(2)}) async-start(), calls=%async_computation.4 | async-start | bytes 4456448 | tf_op jit(solution)/shard_map/reduce_scatter | solution.py:90
  17.9 1.8 copy-start.14
  17.9 1.7 copy-start.16
  17.9 1.7 copy-start.21
  18.8 0.9 copy-start.8
  198.9 1.6 copy-start.1
  200.5 0.7 copy-start.22
  222.8 177.3 %reduce-scatter.5.cloned.1.call-start = ((), (), s32[]{:S(2)}) async-start(), calls=%async_computation.5 | async-start | bytes 6684672 | tf_op jit(solution)/shard_map/reduce_scatter | solution.py:98
  244.1 1.2 copy-start.13
  244.1 2.3 copy-start.9
  244.2 3.3 copy-start.15
  246.5 1.6 copy-start.5
  248.0 54.4 %copy-start.7 = (f32[32,32,256]{2,1,0:T(8,128)S(1)}, f32[32,32,256]{2,1,0:T(8,128)}, u32[]{:S(2)}) copy-start(f32[32,32,256]{2,1,0:T(8,128)} %copy-done.6) | copy-start | bytes 3145732
  248.1 55.5 %copy-start.12 = (bf16[32,32,128]{2,1,0:T(8,128)(2,1)S(1)}, bf16[32,32,128]{2,1,0:T(8,128)(2,1)}, u32[]{:S(2)}) copy-start(bf16[32,32,128]{2,1,0:T(8,128)(2,1)} %param.13) | copy-start | bytes 786436
  248.1 55.5 %copy-start.17 = (bf16[128,256]{1,0:T(8,128)(2,1)S(1)}, bf16[128,256]{1,0:T(8,128)(2,1)}, u32[]{:S(2)}) copy-start(bf16[128,256]{1,0:T(8,128)(2,1)} %param.17) | copy-start | bytes 196612
  250.5 149.7 %copy-start.3 = (f32[32,48,256]{2,1,0:T(8,128)S(1)}, f32[32,48,256]{2,1,0:T(8,128)}, u32[]{:S(2)}) copy-start(f32[32,48,256]{2,1,0:T(8,128)} %copy-done.2) | copy-start | bytes 4718596
  304.4 97.0 %copy-start.11 = (bf16[32,48,128]{2,1,0:T(8,128)(2,1)S(1)}, bf16[32,48,128]{2,1,0:T(8,128)(2,1)}, u32[]{:S(2)}) copy-start(bf16[32,48,128]{2,1,0:T(8,128)(2,1)} %param.14) | copy-start | bytes 1179652
Sparse Core Ops, SparseCore 0:
  13.3 79.7 all-gather.4
  96.4 66.0 all-gather.2
  223.0 79.3 reduce-scatter.2
  306.7 93.3 reduce-scatter.4
where the time goes:
time: 411 us
  waiting for transfers between devices  263 us (64%)
  local copies, waits for them, and re-layouts  74.8 us (18%)
  matrix products  41.4 us (10%)
  other arithmetic  16.9 us (4%)
  between operations  14.2 us (3%)
    reduce_scatter x1, waiting for transfers between devices, per_device(): lax.psum_scatter(jnp.einsum('ijh,kih->kjh', d_triangle, left_full, prefer...  94.3 us
    all_gather x1, waiting for transfers between devices, per_device(): left_full = lax.all_gather(left_gated, 'col', axis=0, tiled=True)  70.1 us
    reduce_scatter x1, waiting for transfers between devices, per_device(): lax.psum_scatter(jnp.einsum('ijh,kjh->kih', d_triangle, right_full, prefe...  51.9 us
    all_gather x1, waiting for transfers between devices, per_device(): right_full = lax.all_gather(right_gated, 'row', axis=0, tiled=True)  46.3 us
    all_gather x1, local copies, waits for them, and re-layouts, per_device(): right_full = lax.all_gather(right_gated, 'row', axis=0, tiled=True)  23.1 us
    all_gather x1, local copies, waits for them, and re-layouts, per_device(): left_full = lax.all_gather(left_gated, 'col', axis=0, tiled=True)  23 us
    dot_general x1, matrix products, per_device(): jnp.einsum('kih,kjh->ijh', left_full, right_full, preferred_element_type=...  13.3 us
    dot_general x1, matrix products, per_device(): jnp.einsum('ijh,kih->kjh', d_triangle, left_full, preferred_element_type=...  11.2 us
  transfers between devices with their start and end apart: 4, of which 4 were waited for; matrix products, arithmetic and copies ran while one was open for 15% of the time, Pallas kernels for 0%

commit v1 on v0

--- a/solution.py
+++ b/solution.py
@@ -67,7 +67,9 @@
     left_gated, left_pre, left_std, left_inv = project(pair_left, ln_gain, ln_bias, w_left)
     right_gated, right_pre, right_std, right_inv = project(pair_right, ln_gain, ln_bias, w_right)
     left_full = lax.all_gather(left_gated, "col", axis=0, tiled=True)
-    right_full = lax.all_gather(right_gated, "row", axis=0, tiled=True)
+    right_full = jnp.concatenate(
+        lax.all_to_all(jnp.stack([right_gated] * lax.axis_size("row")), "row", 0, 0), axis=0
+    )
     triangle = jnp.einsum("kih,kjh->ijh", left_full, right_full, preferred_element_type=jnp.float32)
     tri_normed, tri_std, tri_inv = normalize(triangle, out_gain, out_bias)
     tri_normed = tri_normed.astype(jnp.bfloat16)

time: 411 us -> 392 us (0.954)
  local copies, waits for them, and re-layouts: 74.8 us -> 62.9 us
  matrix products: 41.4 us -> 30.4 us
  starting transfers between devices: 0.56 us -> 8.13 us
    all_to_all x0 -> x1, waiting for transfers between devices: none -> 109 us  [per_device(): lax.all_to_all(jnp.stack([right_gated] * lax.axis_size('row')), 'row', 0, 0)]
    all_gather x1, waiting for transfers between devices: 70.1 us -> 0.01 us  [per_device(): left_full = lax.all_gather(left_gated, 'col', axis=0, tiled=True)]
    all_gather x1 -> x0, waiting for transfers between devices: 46.3 us -> none  [per_device(): right_full = lax.all_gather(right_gated, 'row', axis=0, tiled=True)]
    all_gather x1 -> x0, local copies, waits for them, and re-layouts: 23.1 us -> none  [per_device(): right_full = lax.all_gather(right_gated, 'row', axis=0, tiled=True)]
    reshape x0 -> x1, local copies, waits for them, and re-layouts: none -> 9.68 us  [per_device(): jnp.concatenate(lax.all_to_all(jnp.stack([right_gated] * lax.axis_size('r...]
    all_to_all x0 -> x1, starting transfers between devices: none -> 7.61 us  [per_device(): lax.all_to_all(jnp.stack([right_gated] * lax.axis_size('row')), 'row', 0, 0)]
    dot_general x1, matrix products: 10.8 us -> 3.16 us  [per_device(): jnp.einsum('ijh,kjh->kih', d_triangle, right_full, preferred_element_type...]
    reduce_scatter x1, waiting for transfers between devices: 51.9 us -> 56.9 us  [per_device(): lax.psum_scatter(jnp.einsum('ijh,kjh->kih', d_triangle, right_full, prefe...]
  transfers between devices with their start and end apart: 4 -> 4, of which waited for: 4 -> 3; matrix products, arithmetic and copies ran while one was open for 15% -> 12% of each run, Pallas kernels for 0% -> 0%
where the time goes in v1:
time: 392 us; the launch traced here: 391 us
  waiting for transfers between devices  260 us (66%)
  local copies, waits for them, and re-layouts  62.9 us (16%)
  matrix products  30.4 us (8%)
  other arithmetic  16.2 us (4%)
  between operations  14.2 us (4%)
  starting transfers between devices  8.13 us (2%)
    all_to_all x1, waiting for transfers between devices, per_device(): lax.all_to_all(jnp.stack([right_gated] * lax.axis_size('row')), 'row', 0, 0)  109 us
    reduce_scatter x1, waiting for transfers between devices, per_device(): lax.psum_scatter(jnp.einsum('ijh,kih->kjh', d_triangle, left_full, prefer...  94 us
    reduce_scatter x1, waiting for transfers between devices, per_device(): lax.psum_scatter(jnp.einsum('ijh,kjh->kih', d_triangle, right_full, prefe...  56.9 us
    all_gather x1, local copies, waits for them, and re-layouts, per_device(): left_full = lax.all_gather(left_gated, 'col', axis=0, tiled=True)  23 us
    dot_general x1, matrix products, per_device(): jnp.einsum('ijh,kih->kjh', d_triangle, left_full, preferred_element_type=...  11.2 us
    dot_general x1, matrix products, per_device(): jnp.einsum('kih,kjh->ijh', left_full, right_full, preferred_element_type=...  9.97 us
    dot_general x1, local copies, waits for them, and re-layouts, per_device(): jnp.einsum('ijh,kih->kjh', d_triangle, left_full, preferred_element_type=...  9.91 us
    reshape x1, local copies, waits for them, and re-layouts, per_device(): jnp.concatenate(lax.all_to_all(jnp.stack([right_gated] * lax.axis_size('r...  9.68 us
  transfers between devices with their start and end apart: 4, of which 3 were waited for; matrix products, arithmetic and copies ran while one was open for 12% of the time, Pallas kernels for 0%

profile of v1, /device:TPU:2, one launch (start us, length us, event | category | flops | bytes accessed | tf_op | source)
XLA Modules:
  0.0 391.3 jit_solution(14938557190819078959)
XLA Ops:
  7.2 1.2 convert_reduce_fusion.2
  8.5 1.3 fusion.53
  9.8 1.4 fusion.75
  11.3 1.0 copy-done.5
  12.3 0.8 multiply_convert_fusion.3
  13.2 0.3 convert_reduce_fusion
  13.5 0.5 fusion.20
  14.0 0.6 fusion.68
  14.6 1.1 copy-done.1
  15.8 0.2 multiply_convert_fusion.2
  16.0 3.9 stack.2
  19.9 7.6 %all-to-all-start = ((bf16[16,32,48,128]{3,2,1,0:T(8,128)(2,1)}), bf16[16,32,48,128]{3,2,1,0:T(8,128)(2,1)}, u32[]{:S(2)}, u32[]{:S(2)}) async-start(bf16[16,32,48,128]{3,2,1,0:T(8,128)(2,1)} %stack.2), calls=%async_computation | async-start | bytes 12582912 | tf_op jit(solution)/shard_map/all_to_all | solution.py:71
  27.5 0.2 reduce-scatter.3.cloned.1.call-start
  27.7 0.3 convert_reduce_fusion.1
  28.0 0.5 fusion.27
  28.6 0.5 fusion.22
  29.1 0.4 fusion.2
  29.4 0.1 copy-done.13
  29.5 0.5 multiply_reduce_fusion.2
  30.0 0.3 copy-done.7
  30.3 1.8 copy.33
  32.2 108.6 %all-to-all-done = bf16[16,32,48,128]{3,2,1,0:T(8,128)(2,1)} async-done(((bf16[16,32,48,128]{3,2,1,0:T(8,128)(2,1)}), bf16[16,32,48,128]{3,2,1,0:T(8,128)(2,1)}, u32[]{:S(2)}, u32[]{:S(2)}) %all-to-all-start) | async-done | bytes 6291488 | tf_op jit(solution)/shard_map/all_to_all | solution.py:71
  140.8 9.7 %copy.30 = bf16[512,48,128]{0,1,2:T(8,128)(2,1)} copy(bf16[512,48,128]{2,1,0:T(8,128)(2,1)} %bitcast.2) | data formatting | bytes 12582912 | tf_op jit(solution)/shard_map/reshape | solution.py:70
  150.5 23.0 %copy.36 = bf16[512,32,128]{1,0,2:T(8,128)(2,1)} copy(bf16[512,32,128]{2,1,0:T(8,128)(2,1)} %all-gather.2.cloned.1.call-done) | data formatting | bytes 8388608 | tf_op jit(solution)/shard_map/all_gather | solution.py:69
  173.5 10.0 %bitcast_reduce_fusion = (f32[32,48]{1,0:T(8,128)S(1)}, f32[128,48,32]{1,2,0:T(8,128)S(1)}) fusion(bf16[512,48,128]{0,1,2:T(8,128)(2,1)} %copy.30, bf16[512,32,128]{1,0,2:T(8,128)(2,1)} %copy.36), kind=kOutput, calls=%fused_computation.7 | convolution fusion | flops 201521664 | bytes 11278336 | tf_op jit(solution)/shard_map/kih,kjh->ijh/dot_general | solution.py:73
  183.5 0.3 multiply_reduce_fusion.1
  183.9 0.5 multiply_reduce_fusion
  184.4 0.3 copy-done.21
  184.7 1.8 multiply_convert_fusion
  186.6 3.2 fusion.91
  189.7 9.1 %copy.35 = bf16[128,512,32]{0,2,1:T(8,128)(2,1)} copy(bf16[128,512,32]{1,2,0:T(8,128)(2,1)} %fusion.91) | data formatting | bytes 8388608 | tf_op jit(solution)/shard_map/ijh,kjh->kih/dot_general | solution.py:93
  198.9 0.3 reduce-scatter.5.cloned.1.call-start
  199.1 11.2 %fusion.90 = bf16[128,512,48]{1,2,0:T(8,128)(2,1)} fusion(bf16[512,32,128]{1,0,2:T(8,128)(2,1)} %copy.36, bf16[32,48,128]{1,0,2:T(8,128)(2,1)S(1)} %get-tuple-element.8), kind=kOutput, calls=%fused_computation.132 | convolution fusion | flops 201326592 | bytes 10878976 | tf_op jit(solution)/shard_map/ijh,kih->kjh/dot_general | solution.py:101
  210.4 9.9 %copy.37 = bf16[128,512,48]{0,2,1:T(8,128)(2,1)} copy(bf16[128,512,48]{1,2,0:T(8,128)(2,1)} %fusion.90) | data formatting | bytes 12582912 | tf_op jit(solution)/shard_map/ijh,kih->kjh/dot_general | solution.py:101
  220.3 1.2 copy-done.12
  221.5 1.1 copy.32
  222.6 1.0 multiply_convert_fusion.1
  223.6 0.5 multiply_reduce_fusion.3
  224.2 0.7 fusion.23
  224.9 1.7 fusion.26
  226.6 56.9 %reduce-scatter.3.cloned.1.call-done = bf16[32,32,128]{2,1,0:T(8,128)(2,1)} async-done(((bf16[512,32,128]{2,1,0:T(8,128)(2,1)}), bf16[32,32,128]{2,1,0:T(8,128)(2,1)}) %reduce-scatter.3.cloned.1.call-update) | async-done | bytes 262160 | tf_op jit(solution)/shard_map/reduce_scatter | solution.py:92
  283.5 1.2 fusion.54
  284.7 0.8 fusion.89
  285.5 1.3 fusion.52
  286.8 94.0 %reduce-scatter.5.cloned.1.call-done = bf16[32,48,128]{2,1,0:T(8,128)(2,1)} async-done(((bf16[512,48,128]{2,1,0:T(8,128)(2,1)}), bf16[32,48,128]{2,1,0:T(8,128)(2,1)}) %reduce-scatter.5.cloned.1.call-update) | async-done | bytes 393232 | tf_op jit(solution)/shard_map/reduce_scatter | solution.py:100
  380.9 1.3 fusion.28
  382.2 0.9 fusion.88
  383.2 1.7 fusion.19
  (64 shorter events, 0.4 us)
Async XLA Ops:
  7.2 6.8 %copy-start = (bf16[128,256]{1,0:T(8,128)(2,1)S(1)}, bf16[128,256]{1,0:T(8,128)(2,1)}, u32[]{:S(2)}) copy-start(bf16[128,256]{1,0:T(8,128)(2,1)} %param.18) | copy-start | bytes 196612
  7.2 6.0 %copy-start.9 = (bf16[32,48,128]{2,1,0:T(8,128)(2,1)S(1)}, bf16[32,48,128]{2,1,0:T(8,128)(2,1)}, u32[]{:S(2)}) copy-start(bf16[32,48,128]{2,1,0:T(8,128)(2,1)} %param.14) | copy-start | bytes 1179652
  7.2 143.3 %all-gather.2.cloned.1.call-start = ((), (), s32[]{:S(2)}) async-start(), calls=%async_computation.3 | async-start | bytes 4456448 | tf_op jit(solution)/shard_map/all_gather | solution.py:69
  8.5 5.5 %copy-start.18 = (f32[128]{0:T(128)S(1)}, f32[128]{0:T(128)}, u32[]{:S(2)}) copy-start(f32[128]{0:T(128)} %param.15) | copy-start | bytes 1540
  8.5 5.5 %copy-start.19 = (f32[128]{0:T(128)S(1)}, f32[128]{0:T(128)}, u32[]{:S(2)}) copy-start(f32[128]{0:T(128)} %param.16) | copy-start | bytes 1540
  11.3 1.0 copy-start.5
  14.6 1.2 copy-start.1
  19.9 7.8 %copy-start.3 = (bf16[32,48,128]{2,1,0:T(8,128)(2,1)S(1)}, bf16[32,48,128]{2,1,0:T(8,128)(2,1)}, u32[]{:S(2)}) copy-start(bf16[32,48,128]{2,1,0:T(8,128)(2,1)} %param.12) | copy-start | bytes 1179652
  19.9 9.2 %copy-start.17 = (bf16[128,128]{1,0:T(8,128)(2,1)S(1)}, bf16[128,128]{1,0:T(8,128)(2,1)}, u32[]{:S(2)}) copy-start(bf16[128,128]{1,0:T(8,128)(2,1)} %param.19) | copy-start | bytes 98308
  19.9 121.0 %all-to-all-start = ((bf16[16,32,48,128]{3,2,1,0:T(8,128)(2,1)}), bf16[16,32,48,128]{3,2,1,0:T(8,128)(2,1)}, u32[]{:S(2)}, u32[]{:S(2)}) async-start(bf16[16,32,48,128]{3,2,1,0:T(8,128)(2,1)} %stack.2), calls=%async_computation | async-start | bytes 12582912 | tf_op jit(solution)/shard_map/all_to_all | solution.py:71
  27.5 256.0 %reduce-scatter.3.cloned.1.call-start = ((), (), s32[]{:S(2)}) async-start(), calls=%async_computation.4 | async-start | bytes 4456448 | tf_op jit(solution)/shard_map/reduce_scatter | solution.py:92
  28.5 1.0 copy-start.13
  28.5 1.0 copy-start.15
  28.6 1.0 copy-start.20
  29.4 0.9 copy-start.7
  183.5 3.0 slice-start
  183.9 0.8 copy-start.21
  183.9 2.7 slice-start.1
  198.9 182.0 %reduce-scatter.5.cloned.1.call-start = ((), (), s32[]{:S(2)}) async-start(), calls=%async_computation.5 | async-start | bytes 6684672 | tf_op jit(solution)/shard_map/reduce_scatter | solution.py:100
  220.3 1.2 copy-start.12
  220.3 2.3 copy-start.8
  220.3 3.3 copy-start.14
  222.6 1.6 copy-start.4
  224.1 59.4 %copy-start.6 = (f32[32,32,256]{2,1,0:T(8,128)S(1)}, f32[32,32,256]{2,1,0:T(8,128)}, u32[]{:S(2)}) copy-start(f32[32,32,256]{2,1,0:T(8,128)} %copy-done.5) | copy-start | bytes 3145732
  224.2 60.5 %copy-start.11 = (bf16[32,32,128]{2,1,0:T(8,128)(2,1)S(1)}, bf16[32,32,128]{2,1,0:T(8,128)(2,1)}, u32[]{:S(2)}) copy-start(bf16[32,32,128]{2,1,0:T(8,128)(2,1)} %param.13) | copy-start | bytes 786436
  224.2 60.5 %copy-start.16 = (bf16[128,256]{1,0:T(8,128)(2,1)S(1)}, bf16[128,256]{1,0:T(8,128)(2,1)}, u32[]{:S(2)}) copy-start(bf16[128,256]{1,0:T(8,128)(2,1)} %param.17) | copy-start | bytes 196612
  226.6 154.3 %copy-start.2 = (f32[32,48,256]{2,1,0:T(8,128)S(1)}, f32[32,48,256]{2,1,0:T(8,128)}, u32[]{:S(2)}) copy-start(f32[32,48,256]{2,1,0:T(8,128)} %copy-done.1) | copy-start | bytes 4718596
  285.5 96.7 %copy-start.10 = (bf16[32,48,128]{2,1,0:T(8,128)(2,1)S(1)}, bf16[32,48,128]{2,1,0:T(8,128)(2,1)}, u32[]{:S(2)}) copy-start(bf16[32,48,128]{2,1,0:T(8,128)(2,1)} %param.14) | copy-start | bytes 1179652
Sparse Core Ops, SparseCore 0:
  13.3 102.5 all-gather.1
  199.0 84.4 reduce-scatter.2
  287.9 92.9 reduce-scatter.4
